TPU v7x, 256 devices: a whole 4x4x8 slice. The times are simulated.
256 devices in a mesh: slab: 32 (over z, x), group: 8 (over y, core).
Axes of the slice: x: 4, y: 4, z: 8, core: 2. Of those that a mesh axis runs over, the one named last changes fastest.
Arguments:
- right_side: float32 [64, 32768], P(None, ('slab', 'group')), may hold values from -6 to 6
- fine_blocks: float32 [3, 64, 64, 32768], P(None, None, None, ('slab', 'group')), may hold values from -2 to 4
- fine_inverse: float32 [64, 64, 32768], P(None, None, ('slab', 'group')), may hold values from -0.1 to 0.6
- pattern: int32 [2, 32768], P(None, ('slab', 'group')), may hold values 0 or 1
- tentative: float32 [4, 64, 32768], P(None, None, ('slab', 'group')), may hold values from -5 to 5
- slot_map: int32 [2048, 64], P(('slab', 'group')), may hold values from 0 to 63, each once within a row
- coarse_inverse: float32 [64, 64, 2048], P(None, None, ('slab', 'group')), may hold values from -0.002 to 0.21
- coarse_lower: float32 [64, 64, 2048], P(None, None, ('slab', 'group')), may hold values from -10.1 to 0.1
Outputs:
- solution: float32 [64, 32768], P(None, ('slab', 'group'))
- coarse_error: float32 [64, 2048], P(None, ('slab', 'group'))
All inputs are finite; a program needn't handle non-finite values. No bound on the sum of `pattern` on one device may be relied on, other than what follows from the above.
Results may differ from a plain program's by a relative error of at most 0.0003.
Values sent between devices are 32-bit elements; how exact they have to be, the bound alone decides.
A program may use at most 64 MiB of HBM per device.

v0:
```python
import functools
import math

import jax
import jax.numpy as jnp
from jax import lax
from jax.experimental import pallas as pl
from jax.experimental.pallas import tpu as pltpu
from jax.sharding import PartitionSpec as P

DAMP = 0.8
SMOOTH = 0.67
F32 = jnp.float32
BF16 = jnp.bfloat16
MESH = pl.DeviceIdType.MESH

NN = (((1,), (0,)), ((), ()))
NT = (((1,), (1,)), ((), ()))


def split(x):
    hi = x.astype(BF16)
    return hi, (x - hi.astype(F32)).astype(BF16)


def dot1(a, b, dims=NN):
    return lax.dot_general(a, b, dims, preferred_element_type=F32)


def halves(t):
    n = t.shape[1] // 2
    return t[:, :n] + t[:, n:]


def dotf(a, b, dims=NN):
    return lax.dot_general(a, b, dims, precision=lax.Precision.HIGHEST, preferred_element_type=F32)


def dot2(a, b, dims=NN):
    t = dot1(jnp.concatenate(split(a), axis=0), b, dims)
    return t[: a.shape[0]] + t[a.shape[0] :]


def iota(shape, dim):
    return lax.broadcasted_iota(jnp.int32, shape, dim)


def fold(parts, axis):
    step = 1 if axis == 0 else 16
    at = iota((8, 128), axis) // step

    def mix(a, b, mask, shift):
        return jnp.where(mask, a, b) + pltpu.roll(jnp.where(mask, b, a), shift * step, axis)

    q = [parts[(i + 3) % 8] for i in range(8)]
    y = [mix(q[k], q[k + 4], ((at - k) & 7) < 4, 4) for k in range(4)]
    z = [mix(y[k], y[k + 2], ((at - k) & 3) >= 2, 2) for k in range(2)]
    return mix(z[0], z[1], (at & 1) == 1, 1)


def row_sum(x):
    x = x + pltpu.roll(x, 4, 0)
    x = x + pltpu.roll(x, 2, 0)
    return x + pltpu.roll(x, 1, 0)


def matvec(terms, width, emit):
    turns = 2 if len(terms) > 1 else 4

    def one(g, unused):
        for turn in range(turns):
            first = (g * turns + turn) * 8
            parts = []
            for a in range(8):
                total = None
                for load, v in terms:
                    product = load(first + a) * v
                    total = product if total is None else total + product
                parts.append(jnp.sum(total.reshape(width // 8, 8, 128), axis=0))
            emit(pl.ds(pl.multiple_of(first, 8), 8), fold(parts, 0))
        return unused

    lax.fori_loop(0, width // 8 // turns, one, 0)


def pack_matrix(m):
    return jnp.concatenate([m[:32, :], m[32:, :]], axis=1)


def unpack_matrix(p):
    return jnp.concatenate([p[:, :64], p[:, 64:]], axis=0)


def scan_products(refs, count):
    half = 1
    while half < count:
        for start in range(0, count, 2 * half):
            mid = start + half
            left = pl.ds(start * 64, half * 64)
            for ref in refs:
                ref[left, :] = dotf(ref[left, :], ref[pl.ds(mid * 64, 64), :])
        half *= 2


def scan_prefix(ref, count):
    half = 1
    while half < count:
        for start in range(0, count, 2 * half):
            mid = start + half
            right = pl.ds(mid * 64, half * 64)
            ref[right, :] = dotf(ref[right, :], ref[pl.ds((mid - 1) * 64, 64), :])
        half *= 2


def diagonal(x, count):
    return jnp.where(iota(x.shape, 0) == iota(x.shape, 1) // 64, x, 0.0)


def lanes_folded(x):
    t = x[:, 0:128] + x[:, 128:256] + x[:, 256:384] + x[:, 384:512]
    return t[:, :64] + t[:, 64:]


def padded(x):
    return jnp.concatenate([x, jnp.zeros_like(x)], axis=1)


def kernel(
    nz, nx, ng,
    b_h, f_h, i_h, pat_h, tent_h, slot_h, ci_h, cl_h,
    sol_ref, ce_ref,
    F, I, b, pat, tent, slot, ci, cl,
    work, res, corr,
    cis, Zl, Pl, Z1, Zm1, Z2, Zm2, Zm3,
    Xl, W1, W2, W3,
    RM1, RM2, RM3, RV1, RV2, RV3, halo_out, halo_in,
    Hc, msg, n_mat, vec, n_vec, n_slot, n_first, n_off, off_out, first_out,
    load_sem, m_send, m_recv, v_send, v_recv, h_send, h_recv, n_send, n_recv, f_send, f_recv,
):
    slab, g = lax.axis_index("slab"), lax.axis_index("group")
    z, x = slab // nx, slab % nx
    ns = nz * nx

    def in_group(o):
        return (slab, lax.rem(g + o, ng))

    def along_x(o):
        return (z * nx + lax.rem(x + o, nx), g)

    def along_z(o):
        return (lax.rem(z + o, nz) * nx + x, g)

    at_end, at_start = g == ng - 1, g == 0
    right = (jnp.where(at_end, lax.rem(slab + 1, ns), slab), lax.rem(g + 1, ng))
    left = (jnp.where(at_start, lax.rem(slab + ns - 1, ns), slab), lax.rem(g + ng - 1, ng))

    barrier = pltpu.get_barrier_semaphore()
    peers = [along_z(o) for o in range(1, nz)] + [along_x(o) for o in range(1, nx)] + [right, left]
    peers += [in_group(o) for o in range(1, ng)]
    for peer in peers:
        pl.semaphore_signal(barrier, inc=1, device_id=peer, device_id_type=MESH)

    copies = []
    for k, (src, dst) in enumerate(
        [(ci_h, ci), (cl_h, cl), (i_h, I), (b_h, b), (slot_h, slot), (pat_h, pat),
         (f_h.at[1], F.at[1]), (f_h.at[0], F.at[0]), (f_h.at[2], F.at[2]), (tent_h, tent)]
    ):
        copy = pltpu.make_async_copy(src, dst, load_sem.at[k])
        copy.start()
        copies.append(copy)
    ci_c, cl_c, i_c, b_c, slot_c, pat_c, f1_c, f0_c, f2_c, tent_c = copies

    row64, lane64 = iota((64, 64), 0), iota((64, 64), 1)
    eye = (row64 == lane64).astype(F32)
    ci_c.wait()
    cl_c.wait()
    for j in range(8):
        cij = ci[:, j, :]
        cis[pl.ds(j * 64, 64), :] = cij
        m = -dotf(cij, cl[:, j, :])
        Pl[pl.ds(j * 64, 64), :] = m
        e = m.T
        Zl[pl.ds(j * 64, 64), :] = e
        Xl[pl.ds(j * 64, 64), :] = e
    scan_products([Zl], 8)

    def gather_start(ref, own, target, count, send, recv):
        started = []
        for o in range(1, count):
            copy = pltpu.make_async_remote_copy(
                src_ref=ref.at[own],
                dst_ref=ref.at[own],
                send_sem=send.at[o],
                recv_sem=recv.at[own],
                device_id=target(o),
                device_id_type=MESH,
            )
            copy.start()
            started.append(copy)
        return started

    def gather_wait(started, ref, own, count, recv):
        for o in range(1, count):
            other = lax.rem(own + o, count)
            pltpu.make_async_copy(ref.at[other], ref.at[other], recv.at[other]).wait()
        for copy in started:
            copy.wait_send()

    lane8, lane = iota((8, 128), 1), iota((64, 128), 1)
    has_left = jnp.logical_not(jnp.logical_and(slab == 0, at_start))
    has_right = jnp.logical_not(jnp.logical_and(slab == ns - 1, at_end))

    def halo_pack(turn, ref):
        to_right, to_left = jnp.zeros((8, 128), F32), jnp.zeros((8, 128), F32)
        for k in range(8):
            piece = ref[pl.ds(8 * k, 8), :]
            to_right = jnp.where(lane8 == k, pltpu.roll(piece, k + 1, 1), to_right)
            to_left = jnp.where(lane8 == k, pltpu.roll(piece, k, 1) if k else piece, to_left)
        halo_out[turn, 0] = to_right
        halo_out[turn, 1] = to_left

    def halo_send(turn):
        started = []
        for side, peer in ((0, right), (1, left)):
            copy = pltpu.make_async_remote_copy(
                src_ref=halo_out.at[turn, side],
                dst_ref=halo_in.at[turn, side],
                send_sem=h_send.at[turn, side],
                recv_sem=h_recv.at[turn, side],
                device_id=peer,
                device_id_type=MESH,
            )
            copy.start()
            started.append(copy)
        return started

    def apply_with(value, left_of, right_of, emit):
        before, after = [], []
        for k in range(8):
            piece = value[8 * k : 8 * k + 8]
            before.append(jnp.where(lane8 == 0, left_of(k), pltpu.roll(piece, 1, 1)))
            after.append(jnp.where(lane8 == 127, right_of(k), pltpu.roll(piece, 127, 1)))
        previous = jnp.concatenate(before, axis=0) * pat[0:1, :].astype(F32)
        following = jnp.concatenate(after, axis=0) * pat[1:2, :].astype(F32)
        matvec(
            [
                (lambda a: F[1, a], value),
                (lambda a: F[0, a], previous),
                (lambda a: F[2, a], following),
            ],
            64,
            emit,
        )

    def fine_apply(turn, ref, started, emit):
        for copy in started:
            copy.wait()
        from_left = jnp.where(has_left, halo_in[turn, 0], 0.0)
        from_right = jnp.where(has_right, halo_in[turn, 1], 0.0)

        def left_of(k):
            return pltpu.roll(from_left, 128 - k, 1) if k else from_left

        def right_of(k):
            return pltpu.roll(from_right, 127 - k, 1)

        apply_with(ref[...], left_of, right_of, emit)

    def block_apply(value, emit):
        matvec([(lambda a: I[a], value)], 64, emit)

    def to_residue(rows, y):
        res[rows, :] = b[rows, :] - y

    def sweep(turn, ref, started):
        fine_apply(turn, ref, started, to_residue)

        def emit(rows, y):
            ref[rows, :] = ref[rows, :] + DAMP * y

        block_apply(res[...], emit)

    def first(rows, y):
        work[rows, :] = DAMP * y

    i_c.wait()
    b_c.wait()
    block_apply(b[...], first)
    halo_pack(0, work)

    slot_c.wait()
    q, col = iota((64, 512), 0), iota((64, 512), 1)
    pick = (q == (col % 16) * 4 + col // 128).astype(BF16)
    own_block = iota((8, 512), 0) == (iota((8, 512), 1) % 128) // 16
    slots = dot1(slot[...].astype(F32).astype(BF16), pick)
    slots = row_sum(jnp.where(own_block, slots, 0.0))
    slots = jnp.concatenate([slots] * 8, axis=0)
    GT = (slots == q.astype(F32)).astype(BF16)

    group, spot = lane8 // 16, lane8 % 16
    at_left, at_right = spot < 3, jnp.logical_and(spot >= 8, spot < 11)

    def gather_lanes(pieces, shift, mask, out):
        for k in range(8):
            moved = pltpu.roll(pieces(k), shift + 16 * k, 1)
            out = jnp.where(jnp.logical_and(group == k, mask), moved, out)
        return out

    nothing = jnp.zeros((8, 128), F32)

    def pack_ends(place, pieces):
        vec[0, place] = gather_lanes(pieces, 3, at_left, nothing)
        vec[1, place] = gather_lanes(pieces, 8, at_right, nothing)

    beside = []

    def tell(src, dst, k, peer, send, recv):
        copy = pltpu.make_async_remote_copy(
            src_ref=src, dst_ref=dst, send_sem=send.at[k], recv_sem=recv.at[k], device_id=peer, device_id_type=MESH
        )
        copy.start()
        beside.append(copy)

    def tell_both(src, dst, k, part):
        for side, peer in ((0, right), (1, left)):
            here = src if part is None else src.at[side, part]
            there = dst.at[side] if part is None else dst.at[side, part]
            tell(here, there, k, peer, n_send.at[side], n_recv.at[side])

    first_out[...] = pack_matrix(Pl[0:64, :])
    pack_ends(0, lambda k: b[pl.ds(8 * k, 8), :])
    pat_c.wait()
    tent_c.wait()
    for m in range(4):
        pack_ends(2 + m, lambda k, m=m: tent[m, pl.ds(8 * k, 8), :])
    for r in range(2):
        row = jnp.broadcast_to(pat[r : r + 1, :].astype(F32), (8, 128))
        pack_ends(6 + r, lambda k: row)

    pl.semaphore_wait(barrier, len(peers))

    h0 = halo_send(0)
    RM1[g] = pack_matrix(Zl[0:64, :])
    rm1 = gather_start(RM1, g, in_group, ng, m_send.at[0], m_recv.at[0])

    def gathered(t, load):
        def one(A, unused):
            to_right, to_left = jnp.zeros((8, 128), F32), jnp.zeros((8, 128), F32)
            for u in range(8):
                whole = load(A * 8 + u)
                edge = jnp.zeros((8, 128), F32)
                for k in range(8):
                    piece = pltpu.roll(whole[8 * k : 8 * k + 8], (2 + 16 * k) % 128, 1)
                    edge = jnp.where(lane8 // 16 == k, piece, edge)
                here = (lane8 % 16) // 2 == u
                to_right = jnp.where(here, pltpu.roll(edge, 2 * u, 1) if u else edge, to_right)
                shift = (2 * u - 2) % 128
                to_left = jnp.where(here, pltpu.roll(edge, shift, 1) if shift else edge, to_left)
            msg[0, t, A] = to_right
            msg[1, t, A] = to_left
            return unused

        lax.fori_loop(0, 8, one, 0)

    tell(first_out, n_first, 1, left, f_send, f_recv)
    tell_both(slot, n_slot, 4, None)
    f1_c.wait()
    gathered(1, lambda a: F[1, a])
    tell_both(msg, n_mat, 1, 1)
    f0_c.wait()
    gathered(0, lambda a: F[0, a])
    tell_both(msg, n_mat, 0, 0)
    f2_c.wait()
    sweep(0, work, h0)
    halo_pack(1, work)
    h1 = halo_send(1)

    def upward(started, ref, own, count, recv, full, masked):
        gather_wait(started, ref, own, count, recv)
        for k in range(count):
            e = unpack_matrix(ref[k])
            rows = pl.ds(k * 64, 64)
            if full is not None:
                full[rows, :] = e
            masked[rows, :] = jnp.where(k < own, e, eye)
        scan_products([masked] if full is None else [full, masked], count)

    def later(ref, h, count):
        return ref[pl.ds((h + 1) * 64, 64), :] if h + 1 < count else eye

    upward(rm1, RM1, g, ng, m_recv.at[0], Z1, Zm1)
    RM2[x] = pack_matrix(Z1[0:64, :])
    rm2 = gather_start(RM2, x, along_x, nx, m_send.at[1], m_recv.at[1])
    def weigh(ref, h, parts):
        ref[pl.ds(h * 64, 64), :] = jnp.concatenate(split(jnp.concatenate(parts, axis=1)), axis=1)

    for h in range(ng):
        weigh(W1, h, [later(Z1, h, ng), jnp.where(h < g, later(Zm1, h, ng), 0.0)])

    pack_ends(1, lambda k: work[pl.ds(8 * k, 8), :])
    for side, peer in ((0, right), (1, left)):
        tell(vec.at[side], n_vec.at[side], 5, peer, n_send.at[side], n_recv.at[side])
    gathered(2, lambda a: F[2, a])
    tell_both(msg, n_mat, 2, 2)

    fine_apply(1, work, h1, to_residue)
    residue = res[...]
    values = []
    for m in range(4):
        weight = jnp.sum((tent[m] * residue).reshape(8, 8, 128), axis=0)
        values.append(row_sum(weight) * (1.0 / math.sqrt(64)))
    spread = jnp.where(own_block, jnp.concatenate(values, axis=1), 0.0)
    rhs = dot2(spread, GT, NT)
    offsets = diagonal(dotf(rhs, cis[...], NT), 8)
    after_own = jnp.concatenate([Zl[64:512, :], eye], axis=0)
    RV1[g] = padded(row_sum(dotf(offsets, after_own)))
    rv1 = gather_start(RV1, g, in_group, ng, v_send.at[0], v_recv.at[0])

    upward(rm2, RM2, x, nx, m_recv.at[1], Z2, Zm2)
    RM3[z] = pack_matrix(Z2[0:64, :])
    rm3 = gather_start(RM3, z, along_z, nz, m_send.at[2], m_recv.at[2])
    for h in range(nx):
        weigh(W2, h, [later(Z2, h, nx), jnp.where(h < x, later(Zm2, h, nx), 0.0)])

    own = lanes_folded(offsets)
    off_out[...] = padded(own)
    tell(off_out, n_off, 0, left, f_send, f_recv)
    gathered(3, lambda a: I[a])
    tell_both(msg, n_mat, 3, 3)

    def inflow(ref, weights, count):
        flat = [ref[h] + pltpu.roll(ref[h + 1], 64, 1) for h in range(0, count, 2)]
        return halves(dot2(jnp.concatenate(flat, axis=1), weights[...]))


    gather_wait(rv1, RV1, g, ng, v_recv.at[0])
    flow1 = inflow(RV1, W1, ng)
    RV2[x] = padded(flow1[:, :64])
    rv2 = gather_start(RV2, x, along_x, nx, v_send.at[1], v_recv.at[1])

    scan_prefix(Pl, 8)

    row8 = iota((8, 64), 0)
    carried = jnp.broadcast_to(own[0:1], (8, 64))
    local = carried
    for j in range(1, 8):
        carried = dotf(carried, Xl[pl.ds(j * 64, 64), :]) + own[j : j + 1]
        local = jnp.where(row8 >= j, carried, local)


    gather_wait(rv2, RV2, x, nx, v_recv.at[1])
    flow2 = inflow(RV2, W2, nx)
    RV3[z] = padded(flow2[:, :64])
    rv3 = gather_start(RV3, z, along_z, nz, v_send.at[2], v_recv.at[2])

    upward(rm3, RM3, z, nz, m_recv.at[2], None, Zm3)
    A1 = Zm1[0:64, :]
    A21 = dotf(Zm2[0:64, :], A1)
    for h in range(nz):
        weigh(W3, h, [dotf(jnp.where(h < z, later(Zm3, h, nz), 0.0), A21)])

    nearer = dotf(flow2[:, 64:], A1) + flow1[:, 64:]
    for copy in beside:
        copy.wait()
    valid = jnp.logical_or(jnp.logical_and(at_left, has_left), jnp.logical_and(at_right, has_right))

    def own_ends(ref, out):
        out = gather_lanes(lambda k: ref[pl.ds(8 * k, 8), :], 3, spot == 3, out)
        return gather_lanes(lambda k: ref[pl.ds(8 * k, 8), :], 8, spot == 7, out)

    b_halo, s_halo, *tent_halo = [n_vec[0, k] + n_vec[1, k] for k in range(6)]
    pat_halo = [n_vec[0, k] + n_vec[1, k] for k in (6, 7)]

    def placed(A, unused):
        for t in range(4):
            from_left, from_right = n_mat[0, t, A], n_mat[1, t, A]
            at_two_left = jnp.logical_or(spot == 1, spot == 2)
            at_two_right = jnp.logical_or(spot == 8, spot == 9)
            for u in range(8):
                p = jnp.where(at_two_left, pltpu.roll(from_left, (1 - 2 * u) % 128, 1), 0.0)
                shift = (8 - 2 * u) % 128
                q = pltpu.roll(from_right, shift, 1) if shift else from_right
                Hc[t, A * 8 + u] = jnp.where(at_two_right, q, p)
        return unused

    lax.fori_loop(0, 8, placed, 0)

    place = iota((64, 512), 1) % 16
    asked = jnp.where(place < 3, place + 13, place - 8) * 4 + col // 128
    pick_halo = (q == asked).astype(BF16)
    ends = jnp.concatenate([n_slot[0, 7:8, :], n_slot[1, 0:1, :]] + [n_slot[1, 0:1, :]] * 6, axis=0)
    slots = dot1(ends.astype(F32).astype(BF16), pick_halo)
    which = (iota((8, 512), 1) % 16 >= 8).astype(jnp.int32) == iota((8, 512), 0)
    slots = row_sum(jnp.where(which, slots, 0.0))
    GT_halo = (jnp.concatenate([slots] * 8, axis=0) == q.astype(F32)).astype(BF16)
    M_next = unpack_matrix(n_first[...])
    P_next = dotf(M_next, Pl[448:512, :])
    local_next = dotf(carried, M_next, NT) + n_off[0:1, :64]

    def halo_matvec(terms):
        rows = []
        for A in range(8):
            parts = []
            for u in range(8):
                total = None
                for t, v in terms:
                    term = Hc[t, A * 8 + u] * v
                    total = term if total is None else total + term
                parts.append(total)
            rows.append(fold(parts, 0))
        return fold(rows, 1)

    def halo_apply(v):
        return halo_matvec([(1, v), (0, pltpu.roll(v, 1, 1) * pat_halo[0]), (2, pltpu.roll(v, 127, 1) * pat_halo[1])])

    gather_wait(rv3, RV3, z, nz, v_recv.at[2])
    incoming = inflow(RV3, W3, nz) + nearer

    coarse = local + lanes_folded(diagonal(dotf(incoming, Pl[...], NT), 8))
    ce_ref[...] = coarse
    weights = jnp.where(own_block, dot2(coarse, GT), 0.0)
    total = None
    for m in range(4):
        w = row_sum(weights[:, m * 128 : m * 128 + 128]) * (1.0 / math.sqrt(64))
        term = tent[m] * jnp.concatenate([w] * 8, axis=0)
        total = term if total is None else total + term
    corr[...] = total
    next_first = dotf(incoming, P_next, NT) + local_next
    two = jnp.concatenate([incoming[0:1], next_first[0:1]] + [next_first[0:1]] * 6, axis=0)
    weights = jnp.where(which, dot2(two, GT_halo), 0.0)
    total = None
    for m in range(4):
        w = row_sum(weights[:, m * 128 : m * 128 + 128]) * (1.0 / math.sqrt(64))
        term = tent_halo[m] * w
        total = term if total is None else total + term
    c_halo = own_ends(corr, jnp.where(valid, total, 0.0))

    def post(ref, halo, emit):
        def left_of(k):
            return pltpu.roll(halo, 126 - 16 * k, 1)

        def right_of(k):
            return pltpu.roll(halo, 119 - 16 * k, 1)

        apply_with(ref[...], left_of, right_of, emit)

    def to_res(rows, y):
        res[rows, :] = y

    post(corr, c_halo, to_res)

    def prolong(rows, y):
        sol_ref[rows, :] = work[rows, :] + corr[rows, :] - SMOOTH * y

    block_apply(res[...], prolong)
    s_halo = s_halo + c_halo - SMOOTH * halo_matvec([(3, halo_apply(c_halo))])
    s_halo = jnp.where(valid, s_halo, 0.0)
    s_ends = own_ends(sol_ref, s_halo)

    def smooth(rows, y):
        sol_ref[rows, :] = sol_ref[rows, :] + DAMP * y

    post(sol_ref, s_ends, to_residue)
    block_apply(res[...], smooth)
    s_halo = s_halo + DAMP * halo_matvec([(3, b_halo - halo_apply(s_ends))])
    s_halo = jnp.where(valid, s_halo, 0.0)
    post(sol_ref, s_halo, to_residue)
    block_apply(res[...], smooth)


def body(nz, nx, ng, right_side, fine_blocks, fine_inverse, pattern, tentative, slot_map, coarse_inverse, coarse_lower):
    vmem = lambda *shape: pltpu.VMEM(shape, F32)
    dma = lambda *shape: pltpu.SemaphoreType.DMA(shape)
    top = max(nz, nx, ng)
    scratch = [
        vmem(3, 64, 64, 128), vmem(64, 64, 128), vmem(64, 128), pltpu.VMEM((2, 128), jnp.int32), vmem(4, 64, 128),
        pltpu.VMEM((8, 64), jnp.int32), vmem(64, 8, 64), vmem(64, 8, 64),
        vmem(64, 128), vmem(64, 128), vmem(64, 128),
        vmem(512, 64), vmem(512, 64), vmem(512, 64), vmem(ng * 64, 64), vmem(ng * 64, 64),
        vmem(nx * 64, 64), vmem(nx * 64, 64), vmem(nz * 64, 64),
        vmem(512, 64),
        pltpu.VMEM((ng * 64, 256), BF16), pltpu.VMEM((nx * 64, 256), BF16), pltpu.VMEM((nz * 64, 128), BF16),
        vmem(ng, 32, 128), vmem(nx, 32, 128), vmem(nz, 32, 128),
        vmem(ng, 8, 128), vmem(nx, 8, 128), vmem(nz, 8, 128),
        vmem(2, 2, 8, 128), vmem(2, 2, 8, 128),
        vmem(4, 64, 8, 128), vmem(2, 4, 8, 8, 128), vmem(2, 4, 8, 8, 128), vmem(2, 8, 8, 128), vmem(2, 8, 8, 128),
        pltpu.VMEM((2, 8, 64), jnp.int32), vmem(32, 128), vmem(8, 128), vmem(8, 128), vmem(32, 128),
        dma(10), dma(3, top), dma(3, top), dma(3, top), dma(3, top), dma(2, 2), dma(2, 2),
        dma(2, 6), dma(2, 6), dma(2), dma(2),
    ]
    result, coarse = pl.pallas_call(
        functools.partial(kernel, nz, nx, ng),
        out_shape=(
            jax.ShapeDtypeStruct((64, 128), F32),
            jax.ShapeDtypeStruct((8, 64), F32),
        ),
        in_specs=[pl.BlockSpec(memory_space=pl.ANY)] * 8,
        out_specs=(
            pl.BlockSpec(memory_space=pltpu.VMEM),
            pl.BlockSpec(memory_space=pltpu.VMEM),
        ),
        scratch_shapes=scratch,
        compiler_params=pltpu.CompilerParams(
            collective_id=0, has_side_effects=True, vmem_limit_bytes=60 * 2**20
        ),
        name="v_cycle",
    )(
        right_side, fine_blocks, fine_inverse, pattern, tentative, slot_map,
        jnp.transpose(coarse_inverse, (0, 2, 1)), jnp.transpose(coarse_lower, (0, 2, 1)),
    )
    return result, coarse.T


def solution(mesh):
    slabs, ng = mesh.shape["slab"], mesh.shape["group"]
    nx = 4 if slabs % 4 == 0 and slabs > 4 else 2
    both = ("slab", "group")
    in_specs = (
        P(None, both), P(None, None, None, both), P(None, None, both), P(None, both), P(None, None, both),
        P(both, None), P(None, None, both), P(None, None, both),
    )
    return jax.shard_map(
        functools.partial(body, slabs // nx, nx, ng),
        mesh=mesh,
        in_specs=in_specs,
        out_specs=(P(None, both), P(None, both)),
        check_vma=False,
    )
```

profile of v0, /device:TPU:1, one launch (start us, length us, event | category | flops | bytes accessed | tf_op | source)
XLA Modules:
  0.0 41.5 jit_solution(9485297020036207635)
XLA Ops:
  0.6 38.3 %v_cycle.1 = (f32[64,128]{1,0:T(8,128)}, f32[8,64]{1,0:T(8,128)}) custom-call(f32[64,128]{1,0:T(8,128)} %b_h.1, f32[3,64,64,128]{3,2,1,0:T(8,128)} %f_h.1, f32[64,64,128]{2,1,0:T(8,128)} %i_h.1, s32[2,128]{1,0:T(2,128)} %pat_h.1, f32[4,64,128]{2,1,0:T(8,128)} %tent_h.1, s32[8,64]{1,0:T(8,128)} %slot_h.1, f32[64,8,64]{2,1,0:T(8,128)} %bitcast.3, ...), custom_call_target="tpu_custom_call" | custom-call | tf_op jit(solution)/shard_map/v_cycle/pallas_call | solution.py:591
  38.9 1.4 %copy.12 = f32[64,128]{1,0:T(8,128)} copy(f32[64,128]{1,0:T(8,128)} %get-tuple-element.8) | data formatting | bytes 65536
  40.3 1.3 %copy.13 = f32[64,8]{0,1:T(8,128)} copy(f32[64,8]{0,1:T(8,128)} %bitcast.5) | data formatting | bytes 4096
where the time goes:
time: 41.7 us; the launch traced here: 41.5 us
  Pallas kernels  38.3 us (92%)
  local copies, waits for them, and re-layouts  2.65 us (6%)
  between operations  0.64 us (2%)
    pallas_call x1, Pallas kernels, body(): pl.pallas_call(functools.partial(kernel, nz, nx, ng), out_shape=(jax.Shap...  38.3 us
    unnamed x2, local copies, waits for them, and re-layouts  2.65 us

commit v1 on v0

--- a/solution.py
+++ b/solution.py
@@ -141,6 +141,9 @@
     z, x = slab // nx, slab % nx
     ns = nz * nx
 
+    RM3[...] = jnp.zeros_like(RM3)
+    RV3[...] = jnp.zeros_like(RV3)
+
     def in_group(o):
         return (slab, lax.rem(g + o, ng))
 
@@ -155,8 +158,13 @@
     left = (jnp.where(at_start, lax.rem(slab + ns - 1, ns), slab), lax.rem(g + ng - 1, ng))
 
     barrier = pltpu.get_barrier_semaphore()
-    peers = [along_z(o) for o in range(1, nz)] + [along_x(o) for o in range(1, nx)] + [right, left]
-    peers += [in_group(o) for o in range(1, ng)]
+    for o in range(1, nz):
+
+        @pl.when(z + o >= nz)
+        def _(o=o):
+            pl.semaphore_signal(barrier, inc=1, device_id=along_z(o), device_id_type=MESH)
+
+    peers = [along_x(o) for o in range(1, nx)] + [right, left] + [in_group(o) for o in range(1, ng)]
     for peer in peers:
         pl.semaphore_signal(barrier, inc=1, device_id=peer, device_id_type=MESH)
 
@@ -184,7 +192,13 @@
         Xl[pl.ds(j * 64, 64), :] = e
     scan_products([Zl], 8)
 
-    def gather_start(ref, own, target, count, send, recv):
+    def perhaps(condition, act):
+        if condition is None:
+            act()
+        else:
+            pl.when(condition)(act)
+
+    def gather_start(ref, own, target, count, send, recv, forward=False):
         started = []
         for o in range(1, count):
             copy = pltpu.make_async_remote_copy(
@@ -195,16 +209,18 @@
                 device_id=target(o),
                 device_id_type=MESH,
             )
-            copy.start()
-            started.append(copy)
+            condition = own + o < count if forward else None
+            perhaps(condition, copy.start)
+            started.append((condition, copy))
         return started
 
-    def gather_wait(started, ref, own, count, recv):
+    def gather_wait(started, ref, own, count, recv, forward=False):
         for o in range(1, count):
             other = lax.rem(own + o, count)
-            pltpu.make_async_copy(ref.at[other], ref.at[other], recv.at[other]).wait()
-        for copy in started:
-            copy.wait_send()
+            arrival = pltpu.make_async_copy(ref.at[other], ref.at[other], recv.at[other])
+            perhaps(own + o >= count if forward else None, arrival.wait)
+        for condition, copy in started:
+            perhaps(condition, copy.wait_send)
 
     lane8, lane = iota((8, 128), 1), iota((64, 128), 1)
     has_left = jnp.logical_not(jnp.logical_and(slab == 0, at_start))
@@ -337,7 +353,7 @@
         row = jnp.broadcast_to(pat[r : r + 1, :].astype(F32), (8, 128))
         pack_ends(6 + r, lambda k: row)
 
-    pl.semaphore_wait(barrier, len(peers))
+    pl.semaphore_wait(barrier, len(peers) + nz - 1 - z)
 
     h0 = halo_send(0)
     RM1[g] = pack_matrix(Zl[0:64, :])
@@ -376,7 +392,7 @@
     h1 = halo_send(1)
 
     def upward(started, ref, own, count, recv, full, masked):
-        gather_wait(started, ref, own, count, recv)
+        gather_wait(started, ref, own, count, recv, full is None)
         for k in range(count):
             e = unpack_matrix(ref[k])
             rows = pl.ds(k * 64, 64)
@@ -418,7 +434,7 @@
 
     upward(rm2, RM2, x, nx, m_recv.at[1], Z2, Zm2)
     RM3[z] = pack_matrix(Z2[0:64, :])
-    rm3 = gather_start(RM3, z, along_z, nz, m_send.at[2], m_recv.at[2])
+    rm3 = gather_start(RM3, z, along_z, nz, m_send.at[2], m_recv.at[2], True)
     for h in range(nx):
         weigh(W2, h, [later(Z2, h, nx), jnp.where(h < x, later(Zm2, h, nx), 0.0)])
 
@@ -451,7 +467,7 @@
     gather_wait(rv2, RV2, x, nx, v_recv.at[1])
     flow2 = inflow(RV2, W2, nx)
     RV3[z] = padded(flow2[:, :64])
-    rv3 = gather_start(RV3, z, along_z, nz, v_send.at[2], v_recv.at[2])
+    rv3 = gather_start(RV3, z, along_z, nz, v_send.at[2], v_recv.at[2], True)
 
     upward(rm3, RM3, z, nz, m_recv.at[2], None, Zm3)
     A1 = Zm1[0:64, :]
@@ -513,7 +529,7 @@
     def halo_apply(v):
         return halo_matvec([(1, v), (0, pltpu.roll(v, 1, 1) * pat_halo[0]), (2, pltpu.roll(v, 127, 1) * pat_halo[1])])
 
-    gather_wait(rv3, RV3, z, nz, v_recv.at[2])
+    gather_wait(rv3, RV3, z, nz, v_recv.at[2], True)
     incoming = inflow(RV3, W3, nz) + nearer
 
     coarse = local + lanes_folded(diagonal(dotf(incoming, Pl[...], NT), 8))

time: 41.7 us -> 39.4 us (0.945); the launches traced: 41.5 us -> 38.6 us
  Pallas kernels: 38.3 us -> 35.3 us
    pallas_call x1, Pallas kernels: 38.3 us -> 35.3 us  [body(): pl.pallas_call(functools.partial(kernel, nz, nx, ng), out_shape=(jax.Shap...]
where the time goes in v1:
time: 39.4 us; the launch traced here: 38.6 us
  Pallas kernels  35.3 us (90%)
  local copies, waits for them, and re-layouts  2.65 us (7%)
  between operations  0.64 us (2%)
    pallas_call x1, Pallas kernels, body(): pl.pallas_call(functools.partial(kernel, nz, nx, ng), out_shape=(jax.Shap...  35.3 us
    unnamed x2, local copies, waits for them, and re-layouts  2.65 us

profile of v1, /device:TPU:1, one launch (start us, length us, event | category | flops | bytes accessed | tf_op | source)
XLA Modules:
  0.0 38.6 jit_solution(715798209242920768)
XLA Ops:
  0.6 35.3 %v_cycle.1 = (f32[64,128]{1,0:T(8,128)}, f32[8,64]{1,0:T(8,128)}) custom-call(f32[64,128]{1,0:T(8,128)} %b_h.1, f32[3,64,64,128]{3,2,1,0:T(8,128)} %f_h.1, f32[64,64,128]{2,1,0:T(8,128)} %i_h.1, s32[2,128]{1,0:T(2,128)} %pat_h.1, f32[4,64,128]{2,1,0:T(8,128)} %tent_h.1, s32[8,64]{1,0:T(8,128)} %slot_h.1, f32[64,8,64]{2,1,0:T(8,128)} %bitcast.3, ...), custom_call_target="tpu_custom_call" | custom-call | tf_op jit(solution)/shard_map/v_cycle/pallas_call | solution.py:607
  36.0 1.4 %copy.12 = f32[64,128]{1,0:T(8,128)} copy(f32[64,128]{1,0:T(8,128)} %get-tuple-element.8) | data formatting | bytes 65536
  37.4 1.3 %copy.13 = f32[64,8]{0,1:T(8,128)} copy(f32[64,8]{0,1:T(8,128)} %bitcast.5) | data formatting | bytes 4096

commit v2 on v1

--- a/solution.py
+++ b/solution.py
@@ -192,6 +192,8 @@
         Xl[pl.ds(j * 64, 64), :] = e
     scan_products([Zl], 8)
 
+    sends = []
+
     def perhaps(condition, act):
         if condition is None:
             act()
@@ -219,8 +221,7 @@
             other = lax.rem(own + o, count)
             arrival = pltpu.make_async_copy(ref.at[other], ref.at[other], recv.at[other])
             perhaps(own + o >= count if forward else None, arrival.wait)
-        for condition, copy in started:
-            perhaps(condition, copy.wait_send)
+        sends.extend(started)
 
     lane8, lane = iota((8, 128), 1), iota((64, 128), 1)
     has_left = jnp.logical_not(jnp.logical_and(slab == 0, at_start))
@@ -270,7 +271,8 @@
 
     def fine_apply(turn, ref, started, emit):
         for copy in started:
-            copy.wait()
+            copy.wait_recv()
+            sends.append((None, copy))
         from_left = jnp.where(has_left, halo_in[turn, 0], 0.0)
         from_right = jnp.where(has_right, halo_in[turn, 1], 0.0)
 
@@ -477,7 +479,8 @@
 
     nearer = dotf(flow2[:, 64:], A1) + flow1[:, 64:]
     for copy in beside:
-        copy.wait()
+        copy.wait_recv()
+        sends.append((None, copy))
     valid = jnp.logical_or(jnp.logical_and(at_left, has_left), jnp.logical_and(at_right, has_right))
 
     def own_ends(ref, out):
@@ -582,6 +585,8 @@
     s_halo = jnp.where(valid, s_halo, 0.0)
     post(sol_ref, s_halo, to_residue)
     block_apply(res[...], smooth)
+    for condition, copy in sends:
+        perhaps(condition, copy.wait_send)
 
 
 def body(nz, nx, ng, right_side, fine_blocks, fine_inverse, pattern, tentative, slot_map, coarse_inverse, coarse_lower):

time: 39.4 us -> 39.4 us (level)
  no operation moved by 1% of the time
where the time goes in v2:
time: 39.4 us; the launch traced here: 38.7 us
  Pallas kernels  35.4 us (90%)
  local copies, waits for them, and re-layouts  2.65 us (7%)
  between operations  0.64 us (2%)
    pallas_call x1, Pallas kernels, body(): pl.pallas_call(functools.partial(kernel, nz, nx, ng), out_shape=(jax.Shap...  35.4 us
    unnamed x2, local copies, waits for them, and re-layouts  2.65 us

profile of v2, /device:TPU:1, one launch (start us, length us, event | category | flops | bytes accessed | tf_op | source)
XLA Modules:
  0.0 38.7 jit_solution(8959452253523600364)
XLA Ops:
  0.6 35.4 %v_cycle.1 = (f32[64,128]{1,0:T(8,128)}, f32[8,64]{1,0:T(8,128)}) custom-call(f32[64,128]{1,0:T(8,128)} %b_h.1, f32[3,64,64,128]{3,2,1,0:T(8,128)} %f_h.1, f32[64,64,128]{2,1,0:T(8,128)} %i_h.1, s32[2,128]{1,0:T(2,128)} %pat_h.1, f32[4,64,128]{2,1,0:T(8,128)} %tent_h.1, s32[8,64]{1,0:T(8,128)} %slot_h.1, f32[64,8,64]{2,1,0:T(8,128)} %bitcast.3, ...), custom_call_target="tpu_custom_call" | custom-call | tf_op jit(solution)/shard_map/v_cycle/pallas_call | solution.py:612
  36.0 1.4 %copy.12 = f32[64,128]{1,0:T(8,128)} copy(f32[64,128]{1,0:T(8,128)} %get-tuple-element.8) | data formatting | bytes 65536
  37.4 1.3 %copy.13 = f32[64,8]{0,1:T(8,128)} copy(f32[64,8]{0,1:T(8,128)} %bitcast.5) | data formatting | bytes 4096

commit v3 on v1

--- a/solution.py
+++ b/solution.py
@@ -143,6 +143,7 @@
 
     RM3[...] = jnp.zeros_like(RM3)
     RV3[...] = jnp.zeros_like(RV3)
+    W3[...] = jnp.zeros_like(W3)
 
     def in_group(o):
         return (slab, lax.rem(g + o, ng))
@@ -469,11 +470,20 @@
     RV3[z] = padded(flow2[:, :64])
     rv3 = gather_start(RV3, z, along_z, nz, v_send.at[2], v_recv.at[2], True)
 
-    upward(rm3, RM3, z, nz, m_recv.at[2], None, Zm3)
     A1 = Zm1[0:64, :]
-    A21 = dotf(Zm2[0:64, :], A1)
-    for h in range(nz):
-        weigh(W3, h, [dotf(jnp.where(h < z, later(Zm3, h, nz), 0.0), A21)])
+
+    @pl.when(z > 0)
+    def _():
+        upward(rm3, RM3, z, nz, m_recv.at[2], None, Zm3)
+        A21 = dotf(Zm2[0:64, :], Zm1[0:64, :])
+        for h in range(nz):
+            weigh(W3, h, [dotf(jnp.where(h < z, later(Zm3, h, nz), 0.0), A21)])
+
+    @pl.when(z == 0)
+    def _():
+        for condition, copy in rm3:
+            perhaps(condition, copy.wait_send)
+
 
     nearer = dotf(flow2[:, 64:], A1) + flow1[:, 64:]
     for copy in beside:

time: 39.4 us -> 39.1 us (level)
  the two profiles are of different devices: /device:TPU:1 before, /device:TPU:0 now
where the time goes in v3:
time: 39.1 us; the launch traced here: 39 us
  Pallas kernels  35.7 us (91%)
  local copies, waits for them, and re-layouts  2.65 us (7%)
  between operations  0.64 us (2%)
    pallas_call x1, Pallas kernels, body(): pl.pallas_call(functools.partial(kernel, nz, nx, ng), out_shape=(jax.Shap...  35.7 us
    unnamed x2, local copies, waits for them, and re-layouts  2.65 us

profile of v3, /device:TPU:0, one launch (start us, length us, event | category | flops | bytes accessed | tf_op | source)
XLA Modules:
  0.0 39.0 jit_solution(2176417853192906528)
XLA Ops:
  0.6 35.7 %v_cycle.1 = (f32[64,128]{1,0:T(8,128)}, f32[8,64]{1,0:T(8,128)}) custom-call(f32[64,128]{1,0:T(8,128)} %b_h.1, f32[3,64,64,128]{3,2,1,0:T(8,128)} %f_h.1, f32[64,64,128]{2,1,0:T(8,128)} %i_h.1, s32[2,128]{1,0:T(2,128)} %pat_h.1, f32[4,64,128]{2,1,0:T(8,128)} %tent_h.1, s32[8,64]{1,0:T(8,128)} %slot_h.1, f32[64,8,64]{2,1,0:T(8,128)} %bitcast.3, ...), custom_call_target="tpu_custom_call" | custom-call | tf_op jit(solution)/shard_map/v_cycle/pallas_call | solution.py:617
  36.3 1.4 %copy.12 = f32[64,128]{1,0:T(8,128)} copy(f32[64,128]{1,0:T(8,128)} %get-tuple-element.8) | data formatting | bytes 65536
  37.7 1.3 %copy.13 = f32[64,8]{0,1:T(8,128)} copy(f32[64,8]{0,1:T(8,128)} %bitcast.5) | data formatting | bytes 4096

commit v4 on v3

--- a/solution.py
+++ b/solution.py
@@ -193,6 +193,8 @@
         Xl[pl.ds(j * 64, 64), :] = e
     scan_products([Zl], 8)
 
+    sends = []
+
     def perhaps(condition, act):
         if condition is None:
             act()
@@ -220,8 +222,7 @@
             other = lax.rem(own + o, count)
             arrival = pltpu.make_async_copy(ref.at[other], ref.at[other], recv.at[other])
             perhaps(own + o >= count if forward else None, arrival.wait)
-        for condition, copy in started:
-            perhaps(condition, copy.wait_send)
+        sends.extend(started)
 
     lane8, lane = iota((8, 128), 1), iota((64, 128), 1)
     has_left = jnp.logical_not(jnp.logical_and(slab == 0, at_start))
@@ -478,11 +479,6 @@
         A21 = dotf(Zm2[0:64, :], Zm1[0:64, :])
         for h in range(nz):
             weigh(W3, h, [dotf(jnp.where(h < z, later(Zm3, h, nz), 0.0), A21)])
-
-    @pl.when(z == 0)
-    def _():
-        for condition, copy in rm3:
-            perhaps(condition, copy.wait_send)
 
 
     nearer = dotf(flow2[:, 64:], A1) + flow1[:, 64:]
@@ -592,6 +588,8 @@
     s_halo = jnp.where(valid, s_halo, 0.0)
     post(sol_ref, s_halo, to_residue)
     block_apply(res[...], smooth)
+    for condition, copy in sends:
+        perhaps(condition, copy.wait_send)
 
 
 def body(nz, nx, ng, right_side, fine_blocks, fine_inverse, pattern, tentative, slot_map, coarse_inverse, coarse_lower):

time: 39.1 us -> 39.2 us (level)
  no operation moved by 1% of the time
where the time goes in v4:
time: 39.2 us; the launch traced here: 39 us
  Pallas kernels  35.7 us (91%)
  local copies, waits for them, and re-layouts  2.65 us (7%)
  between operations  0.64 us (2%)
    pallas_call x1, Pallas kernels, body(): pl.pallas_call(functools.partial(kernel, nz, nx, ng), out_shape=(jax.Shap...  35.7 us
    unnamed x2, local copies, waits for them, and re-layouts  2.65 us

profile of v4, /device:TPU:0, one launch (start us, length us, event | category | flops | bytes accessed | tf_op | source)
XLA Modules:
  0.0 39.0 jit_solution(45331658561843243)
XLA Ops:
  0.6 35.7 %v_cycle.1 = (f32[64,128]{1,0:T(8,128)}, f32[8,64]{1,0:T(8,128)}) custom-call(f32[64,128]{1,0:T(8,128)} %b_h.1, f32[3,64,64,128]{3,2,1,0:T(8,128)} %f_h.1, f32[64,64,128]{2,1,0:T(8,128)} %i_h.1, s32[2,128]{1,0:T(2,128)} %pat_h.1, f32[4,64,128]{2,1,0:T(8,128)} %tent_h.1, s32[8,64]{1,0:T(8,128)} %slot_h.1, f32[64,8,64]{2,1,0:T(8,128)} %bitcast.3, ...), custom_call_target="tpu_custom_call" | custom-call | tf_op jit(solution)/shard_map/v_cycle/pallas_call | solution.py:615
  36.4 1.4 %copy.12 = f32[64,128]{1,0:T(8,128)} copy(f32[64,128]{1,0:T(8,128)} %get-tuple-element.8) | data formatting | bytes 65536
  37.7 1.3 %copy.13 = f32[64,8]{0,1:T(8,128)} copy(f32[64,8]{0,1:T(8,128)} %bitcast.5) | data formatting | bytes 4096
